TPU v7x, 32 devices: a whole 2x2x4 slice. The times are simulated.
32 devices in a mesh: dp: 4 (over y, x), vocab: 8 (over z, core).
Axes of the slice: x: 2, y: 2, z: 4, core: 2. Of those that a mesh axis runs over, the one named last changes fastest.
Arguments:
- features: bfloat16 [2048, 4096], P(('dp', 'vocab')), may hold values from -8 to 8
- head: bfloat16 [8192, 4096], P(('dp', 'vocab')), may hold values from -0.5 to 0.5
- momentum: bfloat16 [8192, 4096], P(('dp', 'vocab')), may hold values from -4.5597553e-06 to 4.5597553e-06
- hessian: bfloat16 [8192, 4096], P(('dp', 'vocab')), may hold values from 3.0500814e-08 to 0.00030517578
- true_labels: int32 [2048], replicated, may hold values from 0 to 8191
- sampled_labels: int32 [2048], replicated, may hold values from 0 to 8191
Outputs:
- mean_loss: float32 [], replicated
- new_hessian: bfloat16 [8192, 4096], P(('dp', 'vocab'))
- update: bfloat16 [8192, 4096], P(('dp', 'vocab'))
All inputs are finite; a program needn't handle non-finite values.
Results may differ from a plain program's by a relative error of at most 0.019.
Values may be sent and summed in bfloat16 or wider, within the bound.
No kernel may reach another device: no remote copies, remote signals or barrier semaphores. Data moves between devices by JAX's collectives and lax.ppermute only.
A program may use at most 128 MiB of HBM per device.

v0:
```python
import jax
import jax.numpy as jnp
from jax import lax
from jax.sharding import PartitionSpec as P

hess_decay = 0.99
clip_scale = 0.05


def local_stats(logits, columns, labels):
    highest = jnp.max(logits, axis=1)
    row_total = jnp.sum(jnp.exp(logits - highest[:, None]), axis=1)
    picked = jnp.sum(jnp.where(columns[None, :] == labels[:, None], logits, 0.0), axis=1)
    return (highest, row_total, picked)


def make_signal(logits, log_norm, columns, labels):
    chosen = (columns[None, :] == labels[:, None]).astype(jnp.float32)
    return (jnp.exp(logits - log_norm[:, None]) - chosen).astype(jnp.bfloat16)


def sophia_tail(gradient, momentum, hessian):
    fresh = hess_decay * hessian.astype(jnp.float32) + (1.0 - hess_decay) * gradient * gradient
    clipped = jnp.clip(momentum.astype(jnp.float32) / (clip_scale * fresh), -1.0, 1.0)
    return (fresh.astype(jnp.bfloat16), clipped.astype(jnp.bfloat16))


def shards(features, head, momentum, hessian, true_labels, sampled_labels):
    voc_dev = head.shape[0]
    every_row = lax.all_gather(features, ("dp", "vocab"), axis=0, tiled=True)
    logits = lax.dot_general(
        every_row, head, (((1,), (1,)), ((), ())), preferred_element_type=jnp.float32
    )
    own_offset = (lax.axis_index("dp") * lax.axis_size("vocab") + lax.axis_index("vocab")) * voc_dev
    columns = own_offset + jnp.arange(voc_dev, dtype=jnp.int32)
    highest, row_total, picked = local_stats(logits, columns, true_labels)
    top_all = lax.pmax(highest, ("dp", "vocab"))
    row_total, picked = lax.psum((row_total * jnp.exp(highest - top_all), picked), ("dp", "vocab"))
    highest = top_all
    log_norm = highest + jnp.log(row_total)
    mean_loss = jnp.mean(log_norm - picked)
    signal = make_signal(logits, log_norm, columns, sampled_labels)
    groups = lax.axis_size("dp")
    signal_groups = signal.reshape(groups, -1, voc_dev)
    row_groups = every_row.reshape(groups, -1, every_row.shape[1])
    partials = lax.dot_general(
        signal_groups, row_groups, (((1,), (1,)), ((0,), (0,))), preferred_element_type=jnp.float32
    )
    rounded = lax.optimization_barrier(partials.astype(jnp.bfloat16)).astype(jnp.float32)
    gradient = jnp.sum(rounded, axis=0)
    fresh, clipped = sophia_tail(gradient, momentum, hessian)
    return (mean_loss, fresh, clipped)


def solution(mesh):
    in_specs = (
        P(("dp", "vocab"), None),
        P(("dp", "vocab"), None),
        P(("dp", "vocab"), None),
        P(("dp", "vocab"), None),
        P(),
        P(),
    )
    out_specs = (P(), P(("dp", "vocab"), None), P(("dp", "vocab"), None))
    return jax.shard_map(shards, mesh=mesh, in_specs=in_specs, out_specs=out_specs, check_vma=False)
```

profile of v0, /device:TPU:0, one launch (start us, length us, event | category | flops | bytes accessed | tf_op | source)
XLA Modules:
  0.0 258.7 jit_solution(11792043902208400609)
XLA Ops:
  7.2 0.0 copy-start
  7.2 0.0 all-gather.2.cloned.1.call-start
  7.2 0.7 all-gather.2.cloned.1.call-update
  7.9 0.0 copy-start.1
  7.9 120.7 %all-gather.2.cloned.1.call-done = bf16[2048,4096]{1,0:T(8,128)(2,1)} async-done(((bf16[64,4096]{1,0:T(8,128)(2,1)}), bf16[2048,4096]{1,0:T(8,128)(2,1)}) %all-gather.2.cloned.1.call-update) | async-done | bytes 16777232 | tf_op jit(solution)/shard_map/all_gather | solution.py:30
  128.7 0.0 copy-done
  128.7 9.8 %fusion.2 = (f32[2048]{0:T(1024)S(1)}, f32[2048,256]{1,0:T(8,128)}) fusion(bf16[2048,4096]{1,0:T(8,128)(2,1)} %all-gather.2.cloned.1.call-done, bf16[256,4096]{1,0:T(8,128)(2,1)S(1)} %copy-done), kind=kOutput, calls=%fused_computation.13 | convolution fusion | flops 4295489536 | bytes 20979712 | tf_op jit(solution)/shard_map/dot_general | solution.py:31
  138.5 0.0 copy-start.2
  138.5 38.4 %pmax.7 = f32[2048]{0:T(1024)S(1)} all-reduce(f32[2048]{0:T(1024)S(1)} %get-tuple-element.11), channel_id=1, replica_groups=mesh['dp'=4,'vocab'=8] {'dp','vocab'}, use_global_device_ids=true, to_apply=%region_1.0 | all-reduce | flops 2048 | bytes 16384 | tf_op jit(solution)/shard_map/pmax | solution.py:37
  176.9 0.0 copy-done.1
  176.9 2.5 select_reduce_fusion
  179.5 41.0 %all-reduce = (f32[2048]{0:T(1024)S(1)}, f32[2048]{0:T(1024)S(1)}) all-reduce(f32[2048]{0:T(1024)S(1)} %exponential_multiply_fusion, f32[2048]{0:T(1024)S(1)} %get-tuple-element.3), channel_id=1, replica_groups=mesh['dp'=4,'vocab'=8] {'dp','vocab'}, use_global_device_ids=true, to_apply=%region_3.4 | all-reduce | flops 4096 | bytes 32768 | tf_op jit(solution)/shard_map/psum | solution.py:38
  220.5 0.6 subtract_reduce_fusion
  221.1 0.0 copy-done.2
  221.1 1.9 subtract_convert_fusion
  223.0 12.6 %convolution_convert_fusion = bf16[4,256,4096]{2,1,0:T(8,128)(2,1)} fusion(bf16[4,512,256]{2,1,0:T(8,128)(2,1)S(1)} %bitcast.7, bf16[4,512,4096]{2,1,0:T(8,128)(2,1)} %bitcast.6), kind=kOutput, calls=%fused_computation.1 | convolution fusion | flops 4299161600 | bytes 26214400 | tf_op jit(solution)/shard_map/dot_general | solution.py:46
  235.6 7.3 %convert_reduce_fusion = f32[256,4096]{1,0:T(8,128)} fusion(bf16[4,256,4096]{2,1,0:T(8,128)(2,1)} %convolution_convert_fusion), kind=kLoop, calls=%fused_computation | loop fusion | flops 7340032 | bytes 12582912 | tf_op jit(solution)/shard_map/reduce_sum | solution.py:50
  243.6 7.1 %clamp_convert_fusion = (bf16[256,4096]{1,0:T(8,128)(2,1)}, bf16[256,4096]{1,0:T(8,128)(2,1)}) fusion(bf16[256,4096]{1,0:T(8,128)(2,1)} %param.8, f32[256,4096]{1,0:T(8,128)} %convert_reduce_fusion, bf16[256,4096]{1,0:T(8,128)(2,1)} %param.9), kind=kLoop, calls=%fused_computation.4 | loop fusion | flops 11534336 | bytes 12582912 | tf_op jit(solution)/shard_map/convert_element_type | solution.py:25
  (2 shorter events, 0.0 us)
Async XLA Ops:
  7.2 121.5 %copy-start = (bf16[256,4096]{1,0:T(8,128)(2,1)S(1)}, bf16[256,4096]{1,0:T(8,128)(2,1)}, u32[]{:S(2)}) copy-start(bf16[256,4096]{1,0:T(8,128)(2,1)} %param.7) | copy-start | bytes 6291460
  7.2 121.5 %all-gather.2.cloned.1.call-start = ((), (), s32[]{:S(2)}) async-start(), calls=%async_computation | async-start | bytes 17301504 | tf_op jit(solution)/shard_map/all_gather | solution.py:30
  7.9 169.0 %copy-start.1 = (s32[2048]{0:T(1024)S(1)}, s32[2048]{0:T(1024)}, u32[]{:S(2)}) copy-start(s32[2048]{0:T(1024)} %param.10) | copy-start | bytes 24580
  138.5 82.6 %copy-start.2 = (s32[2048]{0:T(1024)S(1)}, s32[2048]{0:T(1024)}, u32[]{:S(2)}) copy-start(s32[2048]{0:T(1024)} %param.11) | copy-start | bytes 24580
Sparse Core Ops, SparseCore 0:
  11.0 117.5 all-gather.1
where the time goes:
time: 259 us
  waiting for transfers between devices  121 us (47%)
  blocking collectives  79.4 us (31%)
  matrix products  22.5 us (9%)
  other arithmetic  19.5 us (8%)
  between operations  15.9 us (6%)
    all_gather x1, waiting for transfers between devices, shards(): every_row = lax.all_gather(features, ('dp', 'vocab'), axis=0, tiled=True)  121 us
    psum x1, blocking collectives, shards(): lax.psum((row_total * jnp.exp(highest - top_all), picked), ('dp', 'vocab'))  41 us
    pmax x1, blocking collectives, shards(): top_all = lax.pmax(highest, ('dp', 'vocab'))  38.4 us
    dot_general x1, matrix products, shards(): lax.dot_general(signal_groups, row_groups, (((1,), (1,)), ((0,), (0,))),...  12.6 us
    dot_general x1, matrix products, shards(): lax.dot_general(every_row, head, (((1,), (1,)), ((), ())), preferred_elem...  9.85 us
    reduce_sum x1, other arithmetic, shards(): gradient = jnp.sum(rounded, axis=0)  7.29 us
    convert_element_type x1, other arithmetic, sophia_tail(): return (fresh.astype(jnp.bfloat16), clipped.astype(jnp.bfloat16))  7.12 us
  transfers between devices with their start and end apart: 1, of which 1 were waited for; matrix products, arithmetic and copies ran while one was open for 0% of the time, Pallas kernels for 0%

commit v1 on v0

v1 whole, which is shorter than its diff:
```python
import functools

import jax
import jax.numpy as jnp
from jax import lax
from jax.experimental import pallas as pl
from jax.experimental.pallas import tpu as pltpu
from jax.sharding import Mesh, PartitionSpec as P

hess_decay = 0.99
clip_scale = 0.05
N_BLOCKS = 4
PARTS = 2
K_TILE = 2048
LANES = 2
OWNER = 4
OWN = OWNER + N_BLOCKS
C_TILE = 2048
T_TILE = 256
VMEM = 24 * 2**20


def from_all(value, axis, size):
    if size > N_BLOCKS:
        return list(lax.all_gather(value, axis))
    others = [lax.ppermute(value, axis, [(i, (i + s) % size) for i in range(size)]) for s in range(1, size)]
    return [value] + others


whole = pl.BlockSpec(memory_space=pltpu.VMEM)
scalars = pl.BlockSpec(memory_space=pltpu.SMEM)
anywhere = pl.BlockSpec(memory_space=pl.ANY)


def assemble_kernel(plan, *refs):
    outs = refs[-len(plan) :]
    for out, parts in zip(outs, plan):
        at = 0
        for index, begin, size in parts:
            out[at : at + size] = refs[index][begin : begin + size]
            at += size


def assemble(wanted, after=()):
    arrays, plan = [], []
    for parts in wanted:
        plan.append([])
        for array, begin, size in parts:
            places = [i for i, known in enumerate(arrays) if known is array]
            if not places:
                arrays.append(array)
            plan[-1].append((places[0] if places else len(arrays) - 1, begin, size))
    shapes = [(sum(part[2] for part in parts), arrays[0].shape[1]) for parts in plan]
    return pl.pallas_call(
        functools.partial(assemble_kernel, plan),
        in_specs=[whole] * len(arrays) + [anywhere] * len(after),
        out_specs=[whole] * len(shapes),
        out_shape=[jax.ShapeDtypeStruct(shape, jnp.bfloat16) for shape in shapes],
        compiler_params=pltpu.CompilerParams(vmem_limit_bytes=VMEM),
        cost_estimate=pl.CostEstimate(
            flops=0, bytes_accessed=4 * sum(r * w for r, w in shapes), transcendentals=0
        ),
    )(*arrays, *after)


def prepare_kernel(voc_dev, true, sampled, place, *ordered):
    dp, z, core = lax.axis_index("dp"), lax.axis_index("z"), lax.axis_index("core")
    for mask in range(OWNER):
        place[mask] = dp ^ mask
    for k in range(N_BLOCKS):
        place[OWNER + k] = lax.rem(z - k + N_BLOCKS, N_BLOCKS)
    base = (dp * N_BLOCKS + z) * 2
    place[OWN] = (base + core) * voc_dev
    place[OWN + 1] = (base + 1 - core) * voc_dev
    n_dp, chunks = OWNER, 2 * LANES
    width = true.shape[1]
    owner = lax.broadcasted_iota(jnp.int32, (N_BLOCKS, width), 1) // (width // n_dp)
    for labels, out in zip((true, sampled), ordered):
        turned = [pltpu.roll(labels[...], i * (width // chunks), 1) if i else labels[...] for i in range(chunks)]
        for lane in range(LANES):
            found = jnp.zeros((N_BLOCKS, width), jnp.int32)
            for d in range(n_dp):
                rows = slice(d * N_BLOCKS, (d + 1) * N_BLOCKS)
                by_core = [turned[(d - c * LANES - lane) % chunks][rows] for c in range(2)]
                found = jnp.where(owner == d, jnp.where(core == 0, *by_core), found)
            for b in range(N_BLOCKS):
                out[b, lane] = found[b : b + 1]


def prepare(true, sampled, voc_dev):
    tokens = true.shape[0] // 2 // N_BLOCKS // LANES
    return pl.pallas_call(
        functools.partial(prepare_kernel, voc_dev),
        in_specs=[whole] * 2,
        out_specs=[scalars, whole, whole],
        out_shape=[jax.ShapeDtypeStruct((OWN + 2,), jnp.int32)]
        + [jax.ShapeDtypeStruct((N_BLOCKS, LANES, 1, tokens), jnp.int32)] * 2,
        compiler_params=pltpu.CompilerParams(vmem_limit_bytes=VMEM),
        cost_estimate=pl.CostEstimate(flops=0, bytes_accessed=0, transcendentals=0),
    )(true.reshape(-1, tokens), sampled.reshape(-1, tokens))


def logits_kernel(groups, count, place, true, *rest):
    arrays, (head, head_other) = rest[:count], rest[count : count + 2]
    *table, rows, logits, stats, tops = rest[count + 2 :]
    voc, width = head.shape
    tokens = rows.shape[0] // len(groups)
    for number, (_, _, pieces) in enumerate(groups):
        for index, size, begin, slot, offset in pieces:
            start = number * tokens + offset
            if slot is not None:
                start = pl.multiple_of(start + place[slot] * (tokens // 4), 16)
            rows[pl.ds(start, size), :] = arrays[index][begin : begin + size]
    tile = min(K_TILE, width)
    for start in range(0, width, tile):
        columns = slice(start, start + tile)
        both = jnp.concatenate([head[:, columns], head_other[:, columns]], axis=0)
        found = lax.dot_general(
            both, rows[:, columns], (((1,), (1,)), ((), ())), preferred_element_type=jnp.float32
        )
        if start == 0:
            logits[...] = found
        else:
            logits[...] += found
    stats[...] = table[0][...] if table else jnp.zeros_like(stats)
    ids = lax.broadcasted_iota(jnp.int32, (voc, tokens), 0)
    for number, (block, lane, _) in enumerate(groups):
        values = logits[:, number * tokens : (number + 1) * tokens]
        highest = jnp.max(values, axis=0, keepdims=True)
        raised = jnp.exp(values - highest)
        total = jnp.sum(raised, axis=0, keepdims=True)
        owner = place[OWNER + block]
        labels = true[owner, lane]
        picked = jnp.where(ids + place[OWN] == labels, values[:voc], 0.0)
        picked += jnp.where(ids + place[OWN + 1] == labels, values[voc:], 0.0)
        stats[owner, lane, 0:1] = highest + jnp.log(total)
        stats[owner, lane, 1:2] = jnp.sum(picked, axis=0, keepdims=True)
        logits[:, number * tokens : (number + 1) * tokens] = raised
        tops[number] = highest


def block_logits(place, true, groups, head, head_other, stats):
    voc, width = head.shape
    tokens = true.shape[3]
    arrays, plan = [], []
    for block, lane, pieces in groups:
        plan.append((block, lane, []))
        for array, *where in pieces:
            known = [i for i, a in enumerate(arrays) if a is array]
            if not known:
                arrays.append(array)
            plan[-1][2].append((known[0] if known else len(arrays) - 1, *where))
    total = len(groups) * tokens
    return pl.pallas_call(
        functools.partial(logits_kernel, plan, len(arrays)),
        in_specs=[scalars] + [whole] * (len(arrays) + 3 + len(stats)),
        out_specs=[whole] * 4,
        out_shape=[
            jax.ShapeDtypeStruct((total, width), jnp.bfloat16),
            jax.ShapeDtypeStruct((2 * voc, total), jnp.float32),
            jax.ShapeDtypeStruct((*true.shape[:2], 2, tokens), jnp.float32),
            jax.ShapeDtypeStruct((len(groups), 1, tokens), jnp.float32),
        ],
        compiler_params=pltpu.CompilerParams(vmem_limit_bytes=VMEM),
        cost_estimate=pl.CostEstimate(
            flops=4 * voc * total * width,
            bytes_accessed=4 * (voc + total) * width,
            transcendentals=2 * voc * total,
        ),
    )(place, true, *arrays, head, head_other, *stats)


def fill_signal(order, place, log_norm, sampled, raised, tops, signal):
    tokens = sampled.shape[3]
    voc = signal.shape[0] // 2
    ids = lax.broadcasted_iota(jnp.int32, (voc, tokens), 0)
    for number, (block, lane) in enumerate(order):
        values = raised[number // LANES]
        here = (number % LANES) * tokens
        owner = place[OWNER + block]
        scale = jnp.exp(tops[number // LANES][number % LANES] - log_norm[owner, lane])
        for i in range(2):
            half = slice(i * voc, (i + 1) * voc)
            chosen = (ids + place[OWN + i] == sampled[owner, lane]).astype(jnp.float32)
            found = values[half, here : here + tokens] * scale - chosen
            signal[half, number * tokens : (number + 1) * tokens] = found.astype(jnp.bfloat16)


def combine(tables):
    norms = [table[:, :, 0:1] for table in tables]
    top = functools.reduce(jnp.maximum, norms)
    return top + jnp.log(sum(jnp.exp(norm - top) for norm in norms)), sum(table[:, :, 1:2] for table in tables)


def combine_kernel(*refs):
    *tables, out = refs
    out[:, :, 0:1], out[:, :, 1:2] = combine(tables)


def combine_call(tables):
    return pl.pallas_call(
        combine_kernel,
        out_shape=jax.ShapeDtypeStruct(tables[0].shape, jnp.float32),
        compiler_params=pltpu.CompilerParams(vmem_limit_bytes=VMEM),
        cost_estimate=pl.CostEstimate(flops=0, bytes_accessed=0, transcendentals=0),
    )(*tables)


def gradient_kernel(part, order, place, *refs):
    if part:
        signal, *rows, keep, send = refs
    else:
        count = len(refs) - 6 - 3 * N_BLOCKS
        found, (sampled, *raised) = refs[:count], refs[count : count + 1 + 2 * N_BLOCKS]
        *rows, keep, send, signal, losses, log_norm = refs[count + 1 + 2 * N_BLOCKS :]
        norms, picks = combine(found)
        log_norm[...] = norms
        losses[...] = norms - picks
        fill_signal(order, place, log_norm, sampled, raised[:N_BLOCKS], raised[N_BLOCKS:], signal)
    voc, width = keep.shape
    tile = min(C_TILE, width)

    @pl.loop(0, width // tile)
    def _(j):
        here = pl.ds(pl.multiple_of(j * tile, tile), tile)
        there = pl.ds(pl.multiple_of(part * width + j * tile, tile), tile)
        block = jnp.concatenate([r[:, there] for r in rows], axis=0)
        found = jnp.dot(signal[...], block, preferred_element_type=jnp.float32)
        keep[:, here] = found[:voc]
        send[:, here] = found[voc:].astype(jnp.bfloat16)


def gradient_part(part, order, place, rows, tables=(), sampled=None, raised=(), tops=(), signal=None):
    tokens, width = rows[0].shape
    count = N_BLOCKS * tokens
    both = signal.shape[0] if part else raised[0].shape[0]
    voc = both // 2
    out_shape = [
        jax.ShapeDtypeStruct((voc, width // PARTS), jnp.float32),
        jax.ShapeDtypeStruct((voc, width // PARTS), jnp.bfloat16),
    ]
    if part:
        inputs = (signal,)
    else:
        inputs = (*tables, sampled, *raised, *tops)
        out_shape += [
            jax.ShapeDtypeStruct((both, count), jnp.bfloat16),
            jax.ShapeDtypeStruct(sampled.shape, jnp.float32),
        ]
    return pl.pallas_call(
        functools.partial(gradient_kernel, part, order),
        in_specs=[scalars] + [whole] * (len(inputs) + len(rows)),
        out_specs=[whole] * len(out_shape),
        out_shape=out_shape,
        scratch_shapes=[] if part else [pltpu.VMEM(sampled.shape, jnp.float32)],
        compiler_params=pltpu.CompilerParams(vmem_limit_bytes=VMEM),
        cost_estimate=pl.CostEstimate(
            flops=2 * both * count * width // PARTS,
            bytes_accessed=2 * count * width // PARTS,
            transcendentals=0 if part else both * count,
        ),
    )(place, *inputs, *rows)


def tail_kernel(part, n_tokens, kept, got, momentum, hessian, *rest):
    *rest, fresh_buf, update_buf, loss_buf, sems = rest
    copies = []
    if n_tokens:
        losses, losses_other = rest[:2]
        *_, fresh_out, update_out, mean_loss = rest
        both = jnp.sum(losses[...] + losses_other[...], axis=(0, 1))
        loss_buf[...] = jnp.sum(both, axis=1, keepdims=True) / n_tokens
        copies.append(pltpu.make_async_copy(loss_buf, mean_loss, sems.at[0, 2]))
        copies[0].start()
    else:
        fresh_out, update_out = rest[-2:]
    width = kept.shape[1]
    tile = min(T_TILE, width)
    for j in range(width // tile):
        here = slice(j * tile, (j + 1) * tile)
        there = pl.ds(part * width + j * tile, tile)
        gradient = kept[:, here] + got[:, here].astype(jnp.float32)
        fresh = hess_decay * hessian[:, there].astype(jnp.float32) + (1.0 - hess_decay) * gradient * gradient
        scaled = momentum[:, there].astype(jnp.float32) * (1.0 / clip_scale)
        clipped = jnp.clip(scaled * pl.reciprocal(fresh, approx=False), -1.0, 1.0)
        fresh_buf[:, here] = fresh.astype(jnp.bfloat16)
        update_buf[:, here] = clipped.astype(jnp.bfloat16)
        for i, (buf, out) in enumerate(((fresh_buf, fresh_out), (update_buf, update_out))):
            copies.append(pltpu.make_async_copy(buf.at[:, here], out.at[:, there], sems.at[j, i]))
            copies[-1].start()
    for copy in copies:
        copy.wait()


def tail_part(part, kept, got, momentum, hessian, losses, n_tokens, earlier):
    voc, width = momentum.shape
    part_width = width // PARTS
    tile = min(T_TILE, part_width)
    out_specs = [anywhere] * 2
    out_shape = [jax.ShapeDtypeStruct((voc, width), jnp.bfloat16)] * 2
    last = part == PARTS - 1
    if last:
        out_specs.append(anywhere)
        out_shape.append(jax.ShapeDtypeStruct((1, 1), jnp.float32))
    else:
        losses = ()
    return pl.pallas_call(
        functools.partial(tail_kernel, part, n_tokens if last else 0),
        in_specs=[whole] * (4 + len(losses)) + [anywhere] * len(earlier),
        out_specs=out_specs,
        out_shape=out_shape,
        scratch_shapes=[pltpu.VMEM((voc, part_width), jnp.bfloat16)] * 2
        + [pltpu.VMEM((1, 1), jnp.float32), pltpu.SemaphoreType.DMA((part_width // tile, 3))],
        input_output_aliases={4 + len(losses) + i: i for i in range(len(earlier))},
        compiler_params=pltpu.CompilerParams(vmem_limit_bytes=VMEM),
        cost_estimate=pl.CostEstimate(
            flops=10 * voc * width // PARTS, bytes_accessed=14 * voc * width // PARTS, transcendentals=0
        ),
    )(kept, got, momentum, hessian, *losses, *earlier)


def gather_rounds(features):
    swap_x, swap_y = ([(i, i ^ m) for i in range(4)] for m in (1, 2))
    up = [(i, (i + 1) % N_BLOCKS) for i in range(N_BLOCKS)]
    down = [(j, i) for i, j in up]
    n = features.shape[0]
    size = n // LANES
    half = size // 2
    column = [features]
    for _ in range(1, N_BLOCKS):
        column.append(lax.ppermute(column[-1], "z", up))
    first = [lax.ppermute(features, "dp", swap) for swap in (swap_x, swap_y)]
    lanes = range(LANES)
    pieces = [[[(block, size, lane * size, 0, 0)] for lane in lanes] for block in column]
    for lane in lanes:
        pieces[0][lane] += [(array, size, lane * size, 1 + i, 0) for i, array in enumerate(first)]
    got = [[(array, lane * size) for array in first] for lane in lanes]
    after = []
    far, done = [], []
    for k in range(1, N_BLOCKS):
        last = k == N_BLOCKS - 1
        if last:
            after += done[:1]
        for lane in lanes:
            main = [(column[k], lane * size, size)]
            (from_x, x_at), (from_y, y_at) = got[lane]
            relayed = last and lane == LANES - 1
            if relayed:
                wanted = [main]
            else:
                wanted = [main + [(from_y, y_at, half)], main + [(from_x, x_at + half, half)]]
            if k == 2 and lane == LANES - 1:
                wanted.append(far)
            found = assemble(wanted, after)
            after = [found[0]]
            if k == 2 and lane == LANES - 1:
                above = lax.ppermute(found[2], "z", down)
            if relayed:
                (part,) = assemble([[(above, lane * size, size)]])
                pieces[k - 1][lane].append((lax.ppermute(part, "z", down), size, 0, 3, 0))
                found = found * 2
            sent = [lax.ppermute(f, "dp", swap) for f, swap in zip(found, (swap_x, swap_y))]
            for i, array in enumerate(sent):
                pieces[k][lane].append((array, size, 0, 1 + i, 0))
                if not relayed:
                    pieces[k - 1][lane].append((array, half, size, 3, i * half))
                if k == 1:
                    far.append((array, size, half))
            got[lane] = [(array, 0) for array in sent]
        if not last:
            done.append((yield [(k - 1, lane, pieces[k - 1][lane]) for lane in lanes]))
    for lane in lanes:
        pieces[-1][lane].append((above, size, lane * size, 3, 0))
        yield [(k, lane, pieces[k][lane]) for k in (N_BLOCKS - 2, N_BLOCKS - 1)]


def shards(features, head, momentum, hessian, true_labels, sampled_labels):
    n_dp, n_z = lax.axis_size("dp"), lax.axis_size("z")
    dp, z, core = lax.axis_index("dp"), lax.axis_index("z"), lax.axis_index("core")
    voc_dev = head.shape[0]
    n_rows = features.shape[0]
    swap_x = [(i, i ^ 1) for i in range(n_dp)]
    swap_y = [(i, i ^ 2) for i in range(n_dp)]
    swap_core = [(0, 1), (1, 0)]

    base = (dp * n_z + z) * 2
    ring = n_z == N_BLOCKS and n_dp == 4 and n_rows == 32 * LANES
    if ring:
        place, true, sampled = prepare(true_labels, sampled_labels, voc_dev)
    else:

        def in_order(labels):
            mine = labels.reshape(n_dp, N_BLOCKS, -1, 2, n_rows)[:, :, :, core]
            mine = mine.reshape(n_dp, N_BLOCKS, LANES, -1)
            return mine.transpose(1, 2, 0, 3).reshape(N_BLOCKS, LANES, 1, -1)

        true, sampled = in_order(true_labels), in_order(sampled_labels)
        owners = range(N_BLOCKS)
        place = jnp.stack(
            [dp, dp ^ 1, dp ^ 2, dp ^ 3, *owners, (base + core) * voc_dev, (base + 1 - core) * voc_dev]
        ).astype(jnp.int32)
    head_other = lax.ppermute(head, "core", swap_core)

    if ring:
        rounds = gather_rounds(features)
    else:
        column = jnp.split(lax.all_gather(features, "z", axis=0, tiled=True), N_BLOCKS, axis=0)
        n = column[0].shape[0]
        size = n // LANES
        column = [lax.all_gather(block, "dp", axis=0, tiled=True) for block in column]
        calls = [
            [
                (k, lane, [(block, size, d * n + lane * size, None, d * size) for d in range(n_dp)])
                for lane in range(LANES)
            ]
            for k, block in enumerate(column)
        ]
    blocks, order, stats, done = [], [], (), None
    for call in range(N_BLOCKS):
        groups = rounds.send(done) if ring else calls[call]
        order += [group[:2] for group in groups]
        *block, table, done = block_logits(place, true, groups, head, head_other, stats)
        blocks.append((*block, done))
        stats = (table,)

    rows, raised, tops = zip(*blocks)
    (stats,) = stats
    tables = from_all(combine_call(from_all(stats, "z", n_z)), "dp", n_dp)

    kept, summed = [], []
    signal = None
    for part in range(PARTS):
        if part:
            keep, send = gradient_part(part, order, place, rows, signal=signal)
        else:
            keep, send, signal, losses = gradient_part(part, order, place, rows, tables, sampled, raised, tops)
        kept.append(keep)
        summed.append(lax.ppermute(send, "core", swap_core))
    losses = (losses, lax.ppermute(losses, "core", swap_core))
    outs = ()
    for part in range(PARTS):
        outs = tail_part(
            part, kept[part], summed[part], momentum, hessian, losses, true_labels.shape[0], outs
        )
    fresh, clipped, mean_loss = outs
    return mean_loss[0, 0], fresh, clipped


def solution(mesh):
    n_dp, n_voc = mesh.shape["dp"], mesh.shape["vocab"]
    fine = Mesh(mesh.devices.reshape(n_dp, n_voc // 2, 2), ("dp", "z", "core"))
    rows = P(("dp", "z", "core"), None)
    return jax.shard_map(
        shards, mesh=fine, in_specs=(rows,) * 4 + (P(), P()), out_specs=(P(), rows, rows), check_vma=False
    )
```

time: 259 us -> 100 us (0.39)
  blocking collectives: 79.4 us -> 0 us
  waiting for transfers between devices: 121 us -> 48.5 us
  starting transfers between devices: 0.04 us -> 31.1 us
  matrix products: 22.5 us -> 0 us
  other arithmetic: 19.5 us -> 0 us
  Pallas kernels: 0 us -> 19.4 us
  between operations: 15.9 us -> 0.95 us
    all_gather x1 -> x0, waiting for transfers between devices: 121 us -> none  [shards(): every_row = lax.all_gather(features, ('dp', 'vocab'), axis=0, tiled=True)]
    ppermute x0 -> x29, waiting for transfers between devices: none -> 48.5 us  [the longest x12 15.8 us: gather_rounds(): lax.ppermute(f, 'dp', swap)]
    psum x1 -> x0, blocking collectives: 41 us -> none  [shards(): lax.psum((row_total * jnp.exp(highest - top_all), picked), ('dp', 'vocab'))]
    pmax x1 -> x0, blocking collectives: 38.4 us -> none  [shards(): top_all = lax.pmax(highest, ('dp', 'vocab'))]
    ppermute x0 -> x29, starting transfers between devices: none -> 31.1 us  [the longest x12 14.2 us: gather_rounds(): lax.ppermute(f, 'dp', swap)]
    dot_general x2 -> x0, matrix products: 22.5 us -> none  [the longest x1 12.6 us: shards(): lax.dot_general(signal_groups, row_groups, (((1,), (1,)), ((0,), (0,))),...]
    pallas_call x0 -> x17, Pallas kernels: none -> 19.4 us  [the longest x4 8.56 us: block_logits(): pl.pallas_call(functools.partial(logits_kernel, plan, len(arrays)), in_sp...]
    reduce_sum x3 -> x0, other arithmetic: 10.4 us -> none  [the longest x1 7.29 us: shards(): gradient = jnp.sum(rounded, axis=0)]
  transfers between devices with their start and end apart: 1 -> 29, of which waited for: 1 -> 19; matrix products, arithmetic and copies ran while one was open for 0% -> 0% of each run, Pallas kernels for 0% -> 12%
where the time goes in v1:
time: 100 us
  waiting for transfers between devices  48.5 us (48%)
  starting transfers between devices  31.1 us (31%)
  Pallas kernels  19.4 us (19%)
    ppermute x12, waiting for transfers between devices, gather_rounds(): lax.ppermute(f, 'dp', swap)  15.8 us
    ppermute x12, starting transfers between devices, gather_rounds(): lax.ppermute(f, 'dp', swap)  14.2 us
    ppermute x2, waiting for transfers between devices, gather_rounds(): first = [lax.ppermute(features, 'dp', swap) for swap in (swap_x, swap_y)]  9.66 us
    pallas_call x4, Pallas kernels, block_logits(): pl.pallas_call(functools.partial(logits_kernel, plan, len(arrays)), in_sp...  8.56 us
    ppermute x6, waiting for transfers between devices, from_all(): lax.ppermute(value, axis, [(i, (i + s) % size) for i in range(size)])  8.54 us
    ppermute x3, waiting for transfers between devices, gather_rounds(): column.append(lax.ppermute(column[-1], 'z', up))  6.78 us
    ppermute x6, starting transfers between devices, from_all(): lax.ppermute(value, axis, [(i, (i + s) % size) for i in range(size)])  6.48 us
    ppermute x1, waiting for transfers between devices, gather_rounds(): above = lax.ppermute(found[2], 'z', down)  6.05 us
  transfers between devices with their start and end apart: 29, of which 19 were waited for; matrix products, arithmetic and copies ran while one was open for 0% of the time, Pallas kernels for 12%

profile of v1, /device:TPU:0, one launch (start us, length us, event | category | flops | bytes accessed | tf_op | source)
XLA Modules:
  0.0 100.0 jit_solution(10904786997369127517)
XLA Ops:
  1.1 2.6 %collective-permute-start.2 = (bf16[64,4096]{1,0:T(8,128)(2,1)}, bf16[64,4096]{1,0:T(8,128)(2,1)S(1)}, u32[]{:S(2)}, u32[]{:S(2)}) collective-permute-start(bf16[64,4096]{1,0:T(8,128)(2,1)} %rest_0_.1), channel_id=1, source_target_pairs={{0,16},{8,24},{16,0},{24,8},{1,17},{9,25},{17,1},{25,9},{2,18},{10... | collective-permute-start | bytes 1572872 | tf_op jit(solution)/shard_map/ppermute | solution.py:332
  3.7 1.6 %collective-permute-start = (bf16[64,4096]{1,0:T(8,128)(2,1)}, bf16[64,4096]{1,0:T(8,128)(2,1)S(1)}, u32[]{:S(2)}, u32[]{:S(2)}) collective-permute-start(bf16[64,4096]{1,0:T(8,128)(2,1)} %rest_0_.1), channel_id=1, source_target_pairs={{0,2},{2,4},{4,6},{6,0},{1,3},{3,5},{5,7},{7,1},{8,10},{10,12},{12... | collective-permute-start | bytes 1572872 | tf_op jit(solution)/shard_map/ppermute | solution.py:331
  5.3 1.5 %collective-permute-start.3 = (bf16[64,4096]{1,0:T(8,128)(2,1)}, bf16[64,4096]{1,0:T(8,128)(2,1)S(1)}, u32[]{:S(2)}, u32[]{:S(2)}) collective-permute-start(bf16[64,4096]{1,0:T(8,128)(2,1)} %rest_0_.1), channel_id=1, source_target_pairs={{0,8},{8,0},{16,24},{24,16},{1,9},{9,1},{17,25},{25,17},{2,10},{10... | collective-permute-start | bytes 1572872 | tf_op jit(solution)/shard_map/ppermute | solution.py:332
  6.8 9.7 %collective-permute-done.2.refs_1_.rest_2_ = bf16[64,4096]{1,0:T(8,128)(2,1)S(1)} collective-permute-done((bf16[64,4096]{1,0:T(8,128)(2,1)}, bf16[64,4096]{1,0:T(8,128)(2,1)S(1)}, u32[]{:S(2)}, u32[]{:S(2)}) %collective-permute-start.2) | collective-permute-done | bytes 524320 | tf_op jit(solution)/shard_map/ppermute | solution.py:332
  16.5 3.4 %collective-permute-done.refs_0_.rest_0_ = bf16[64,4096]{1,0:T(8,128)(2,1)S(1)} collective-permute-done((bf16[64,4096]{1,0:T(8,128)(2,1)}, bf16[64,4096]{1,0:T(8,128)(2,1)S(1)}, u32[]{:S(2)}, u32[]{:S(2)}) %collective-permute-start) | collective-permute-done | bytes 524320 | tf_op jit(solution)/shard_map/ppermute | solution.py:331
  21.4 1.5 %collective-permute-start.6 = (bf16[48,4096]{1,0:T(8,128)(2,1)S(1)}, bf16[48,4096]{1,0:T(8,128)(2,1)S(1)}, u32[]{:S(2)}, u32[]{:S(2)}) collective-permute-start(bf16[48,4096]{1,0:T(8,128)(2,1)S(1)} %get-tuple-element.46.refs_3_), channel_id=1, source_target_pairs={{0,8},{8,0},{16,24},{24,16},{1,9},{9,1},{17,25},{25,17},{2,10},{10... | collective-permute-start | bytes 1179656 | tf_op jit(solution)/shard_map/ppermute | solution.py:362
  23.0 1.6 %collective-permute-start.4 = (bf16[48,4096]{1,0:T(8,128)(2,1)S(1)}, bf16[48,4096]{1,0:T(8,128)(2,1)S(1)}, u32[]{:S(2)}, u32[]{:S(2)}) collective-permute-start(bf16[48,4096]{1,0:T(8,128)(2,1)S(1)} %get-tuple-element.47), channel_id=1, source_target_pairs={{0,16},{8,24},{16,0},{24,8},{1,17},{9,25},{17,1},{25,9},{2,18},{10... | collective-permute-start | bytes 1179656 | tf_op jit(solution)/shard_map/ppermute | solution.py:362
  24.6 7.4 %collective-permute-done.7.refs_1_.refs_4_.rest_4_.rest_2_ = bf16[48,4096]{1,0:T(8,128)(2,1)S(1)} collective-permute-done((bf16[48,4096]{1,0:T(8,128)(2,1)S(1)}, bf16[48,4096]{1,0:T(8,128)(2,1)S(1)}, u32[]{:S(2)}, u32[]{:S(2)}) %collective-permute-start.7) | collective-permute-done | bytes 393248 | tf_op jit(solution)/shard_map/ppermute | solution.py:362
  32.0 1.6 %collective-permute-start.5 = (bf16[48,4096]{1,0:T(8,128)(2,1)S(1)}, bf16[48,4096]{1,0:T(8,128)(2,1)S(1)}, u32[]{:S(2)}, u32[]{:S(2)}) collective-permute-start(bf16[48,4096]{1,0:T(8,128)(2,1)S(1)} %get-tuple-element.48.refs_3_), channel_id=1, source_target_pairs={{0,8},{8,0},{16,24},{24,16},{1,9},{9,1},{17,25},{25,17},{2,10},{10... | collective-permute-start | bytes 1179656 | tf_op jit(solution)/shard_map/ppermute | solution.py:362
  33.6 1.9 %collective-permute-done.1.refs_0_.rest_0_ = bf16[64,4096]{1,0:T(8,128)(2,1)S(1)} collective-permute-done((bf16[64,4096]{1,0:T(8,128)(2,1)S(1)}, bf16[64,4096]{1,0:T(8,128)(2,1)S(1)}, u32[]{:S(2)}, u32[]{:S(2)}) %collective-permute-start.1) | collective-permute-done | bytes 524320 | tf_op jit(solution)/shard_map/ppermute | solution.py:331
  35.5 1.4 %collective-permute-start.13 = (bf16[48,4096]{1,0:T(8,128)(2,1)S(1)}, bf16[48,4096]{1,0:T(8,128)(2,1)S(1)}, u32[]{:S(2)}, u32[]{:S(2)}) collective-permute-start(bf16[48,4096]{1,0:T(8,128)(2,1)S(1)} %get-tuple-element.54), channel_id=1, source_target_pairs={{0,16},{8,24},{16,0},{24,8},{1,17},{9,25},{17,1},{25,9},{2,18},{10... | collective-permute-start | bytes 1179656 | tf_op jit(solution)/shard_map/ppermute | solution.py:362
  36.9 3.5 %collective-permute-done.4.refs_1_.rest_6_ = bf16[48,4096]{1,0:T(8,128)(2,1)S(1)} collective-permute-done((bf16[48,4096]{1,0:T(8,128)(2,1)S(1)}, bf16[48,4096]{1,0:T(8,128)(2,1)S(1)}, u32[]{:S(2)}, u32[]{:S(2)}) %collective-permute-start.4) | collective-permute-done | bytes 393248 | tf_op jit(solution)/shard_map/ppermute | solution.py:362
  40.4 1.5 %collective-permute-start.14 = (bf16[48,4096]{1,0:T(8,128)(2,1)S(1)}, bf16[48,4096]{1,0:T(8,128)(2,1)S(1)}, u32[]{:S(2)}, u32[]{:S(2)}) collective-permute-start(bf16[48,4096]{1,0:T(8,128)(2,1)S(1)} %get-tuple-element.50.refs_5_), channel_id=1, source_target_pairs={{0,8},{8,0},{16,24},{24,16},{1,9},{9,1},{17,25},{25,17},{2,10},{10... | collective-permute-start | bytes 1179656 | tf_op jit(solution)/shard_map/ppermute | solution.py:362
  42.0 2.3 %collective-permute-start.10 = (bf16[64,4096]{1,0:T(8,128)(2,1)S(1)}, bf16[64,4096]{1,0:T(8,128)(2,1)S(1)}, u32[]{:S(2)}, u32[]{:S(2)}) collective-permute-start(bf16[64,4096]{1,0:T(8,128)(2,1)S(1)} %get-tuple-element.53), channel_id=1, source_target_pairs={{2,0},{4,2},{6,4},{0,6},{3,1},{5,3},{7,5},{1,7},{10,8},{12,10},{14... | collective-permute-start | bytes 1572872 | tf_op jit(solution)/shard_map/ppermute | solution.py:357
  44.3 3.0 %collective-permute-done.13.refs_1_.rest_4_.rest_2_ = bf16[48,4096]{1,0:T(8,128)(2,1)S(1)} collective-permute-done((bf16[48,4096]{1,0:T(8,128)(2,1)S(1)}, bf16[48,4096]{1,0:T(8,128)(2,1)S(1)}, u32[]{:S(2)}, u32[]{:S(2)}) %collective-permute-start.13) | collective-permute-done | bytes 393248 | tf_op jit(solution)/shard_map/ppermute | solution.py:362
  48.0 1.3 %collective-permute-start.8 = (bf16[48,4096]{1,0:T(8,128)(2,1)S(1)}, bf16[48,4096]{1,0:T(8,128)(2,1)S(1)}, u32[]{:S(2)}, u32[]{:S(2)}) collective-permute-start(bf16[48,4096]{1,0:T(8,128)(2,1)S(1)} %get-tuple-element.51.refs_3_), channel_id=1, source_target_pairs={{0,8},{8,0},{16,24},{24,16},{1,9},{9,1},{17,25},{25,17},{2,10},{10... | collective-permute-start | bytes 1179656 | tf_op jit(solution)/shard_map/ppermute | solution.py:362
  49.9 2.1 %shard_map.91 = (bf16[256,4096]{1,0:T(8,128)(2,1)S(1)}, f32[512,256]{1,0:T(8,128)S(1)}, f32[4,2,2,128]{3,2,1,0:T(2,128)S(1)}, f32[2,1,128]{2,1,0:T(1,128)S(1)}) custom-call(s32[10]{0:T(128)S(1)} %get-tuple-element.44.place, s32[4,2,1,128]{3,2,1,0:T(1,128)S(1)} %get-tuple-element.45.true, bf16[64,4096]{1,0:T(8,128)(2,1)S(1)} %copy-done.3, ...), custom_call_target="tpu_custom_call" | custom-call | flops 1073741824 | bytes 8388608 | tf_op jit(solution)/shard_map/pallas_call | solution.py:154
  52.1 1.5 %collective-permute-done.12.refs_0_.rest_5_.rest_4_ = bf16[64,4096]{1,0:T(8,128)(2,1)S(1)} collective-permute-done((bf16[64,4096]{1,0:T(8,128)(2,1)S(1)}, bf16[64,4096]{1,0:T(8,128)(2,1)S(1)}, u32[]{:S(2)}, u32[]{:S(2)}) %collective-permute-start.12) | collective-permute-done | bytes 524320 | tf_op jit(solution)/shard_map/ppermute | solution.py:331
  55.7 6.0 %collective-permute-done.10.refs_0_.rest_6_.rest_7_ = bf16[64,4096]{1,0:T(8,128)(2,1)S(1)} collective-permute-done((bf16[64,4096]{1,0:T(8,128)(2,1)S(1)}, bf16[64,4096]{1,0:T(8,128)(2,1)S(1)}, u32[]{:S(2)}, u32[]{:S(2)}) %collective-permute-start.10) | collective-permute-done | bytes 524320 | tf_op jit(solution)/shard_map/ppermute | solution.py:357
  64.2 2.1 %shard_map.94 = (bf16[256,4096]{1,0:T(8,128)(2,1)S(1)}, f32[512,256]{1,0:T(8,128)S(1)}, f32[4,2,2,128]{3,2,1,0:T(2,128)S(1)}, f32[2,1,128]{2,1,0:T(1,128)S(1)}) custom-call(s32[10]{0:T(128)S(1)} %get-tuple-element.44.place, s32[4,2,1,128]{3,2,1,0:T(1,128)S(1)} %get-tuple-element.45.true, bf16[64,4096]{1,0:T(8,128)(2,1)S(1)} %collective-permute-done.refs_0_.rest_0_, ...), custom_call_target="tpu_custom_call" | custom-call | flops 1073741824 | bytes 8388608 | tf_op jit(solution)/shard_map/pallas_call | solution.py:154
  66.6 2.1 %shard_map.95 = (bf16[256,4096]{1,0:T(8,128)(2,1)S(1)}, f32[512,256]{1,0:T(8,128)S(1)}, f32[4,2,2,128]{3,2,1,0:T(2,128)S(1)}, f32[2,1,128]{2,1,0:T(1,128)S(1)}) custom-call(s32[10]{0:T(128)S(1)} %get-tuple-element.44.place, s32[4,2,1,128]{3,2,1,0:T(1,128)S(1)} %get-tuple-element.45.true, bf16[64,4096]{1,0:T(8,128)(2,1)S(1)} %collective-permute-done.1.refs_0_.rest_0_, ...), custom_call_target="tpu_custom_call" | custom-call | flops 1073741824 | bytes 8388608 | tf_op jit(solution)/shard_map/pallas_call | solution.py:154
  68.8 1.3 %collective-permute-done.11.rest_3_ = bf16[32,4096]{1,0:T(8,128)(2,1)S(1)} collective-permute-done((bf16[32,4096]{1,0:T(8,128)(2,1)S(1)}, bf16[32,4096]{1,0:T(8,128)(2,1)S(1)}, u32[]{:S(2)}, u32[]{:S(2)}) %collective-permute-start.11) | collective-permute-done | bytes 262176 | tf_op jit(solution)/shard_map/ppermute | solution.py:360
  71.6 2.1 %shard_map.96 = (bf16[256,4096]{1,0:T(8,128)(2,1)S(1)}, f32[512,256]{1,0:T(8,128)S(1)}, f32[4,2,2,128]{3,2,1,0:T(2,128)S(1)}, f32[2,1,128]{2,1,0:T(1,128)S(1)}) custom-call(s32[10]{0:T(128)S(1)} %get-tuple-element.44.place, s32[4,2,1,128]{3,2,1,0:T(1,128)S(1)} %get-tuple-element.45.true, bf16[64,4096]{1,0:T(8,128)(2,1)S(1)} %collective-permute-done.1.refs_0_.rest_0_, ...), custom_call_target="tpu_custom_call" | custom-call | flops 1073741824 | bytes 8388608 | tf_op jit(solution)/shard_map/pallas_call | solution.py:154
  73.7 2.2 %collective-permute-start.22 = (f32[4,2,2,128]{3,2,1,0:T(2,128)S(1)}, f32[4,2,2,128]{3,2,1,0:T(2,128)S(1)}, u32[]{:S(2)}, u32[]{:S(2)}) collective-permute-start(f32[4,2,2,128]{3,2,1,0:T(2,128)S(1)} %get-tuple-element.61.refs_0_), channel_id=1, source_target_pairs={{0,6},{2,0},{4,2},{6,4},{1,7},{3,1},{5,3},{7,5},{8,14},{10,8},{12,... | collective-permute-start | bytes 24584 | tf_op jit(solution)/shard_map/ppermute | solution.py:26
  77.4 3.1 %collective-permute-done.21.refs_2_ = f32[4,2,2,128]{3,2,1,0:T(2,128)S(1)} collective-permute-done((f32[4,2,2,128]{3,2,1,0:T(2,128)S(1)}, f32[4,2,2,128]{3,2,1,0:T(2,128)S(1)}, u32[]{:S(2)}, u32[]{:S(2)}) %collective-permute-start.21) | collective-permute-done | bytes 8224 | tf_op jit(solution)/shard_map/ppermute | solution.py:26
  81.7 2.1 %collective-permute-start.25 = (f32[4,2,2,128]{3,2,1,0:T(2,128)S(1)}, f32[4,2,2,128]{3,2,1,0:T(2,128)S(1)}, u32[]{:S(2)}, u32[]{:S(2)}) collective-permute-start(f32[4,2,2,128]{3,2,1,0:T(2,128)S(1)} %shard_map.97.refs_0_), channel_id=1, source_target_pairs={{0,24},{8,0},{16,8},{24,16},{1,25},{9,1},{17,9},{25,17},{2,26},{10... | collective-permute-start | bytes 24584 | tf_op jit(solution)/shard_map/ppermute | solution.py:26
  85.4 2.1 %collective-permute-done.24.refs_2_ = f32[4,2,2,128]{3,2,1,0:T(2,128)S(1)} collective-permute-done((f32[4,2,2,128]{3,2,1,0:T(2,128)S(1)}, f32[4,2,2,128]{3,2,1,0:T(2,128)S(1)}, u32[]{:S(2)}, u32[]{:S(2)}) %collective-permute-start.24) | collective-permute-done | bytes 8224 | tf_op jit(solution)/shard_map/ppermute | solution.py:26
  87.4 1.3 %collective-permute-done.23.refs_1_ = f32[4,2,2,128]{3,2,1,0:T(2,128)S(1)} collective-permute-done((f32[4,2,2,128]{3,2,1,0:T(2,128)S(1)}, f32[4,2,2,128]{3,2,1,0:T(2,128)S(1)}, u32[]{:S(2)}, u32[]{:S(2)}) %collective-permute-start.23) | collective-permute-done | bytes 8224 | tf_op jit(solution)/shard_map/ppermute | solution.py:26
  88.8 3.0 %shard_map.98 = (f32[256,2048]{1,0:T(8,128)S(1)}, bf16[256,2048]{1,0:T(8,128)(2,1)S(1)}, bf16[512,1024]{1,0:T(8,128)(2,1)S(1)}, f32[4,2,1,128]{3,2,1,0:T(1,128)S(1)}) custom-call(s32[10]{0:T(128)S(1)} %get-tuple-element.44.place, f32[4,2,2,128]{3,2,1,0:T(2,128)S(1)} %shard_map.97.refs_0_, f32[4,2,2,128]{3,2,1,0:T(2,128)S(1)} %collective-permute-done.23.refs_1_, ...), custom_call_target="tpu_custom_call" | custom-call | flops 2147483648 | bytes 4194304 | tf_op jit(solution)/shard_map/pallas_call | solution.py:250
  91.8 2.9 %shard_map.99 = (f32[256,2048]{1,0:T(8,128)S(1)}, bf16[256,2048]{1,0:T(8,128)(2,1)S(1)}) custom-call(s32[10]{0:T(128)S(1)} %get-tuple-element.44.place, bf16[512,1024]{1,0:T(8,128)(2,1)S(1)} %get-tuple-element.74.refs_0_, bf16[256,4096]{1,0:T(8,128)(2,1)S(1)} %get-tuple-element.70.refs_13_.refs_1_, bf16[256,4096]{1,0:T(8,128)(2,1)S(1)} %get-tuple-element.71.refs_14_.refs_2_, ...), custom_call_target="tpu_custom_call" | custom-call | flops 2147483648 | bytes 4194304 | tf_op jit(solution)/shard_map/pallas_call | solution.py:250
  95.4 1.8 %shard_map.100 = (bf16[256,4096]{1,0:T(8,128)(2,1)}, bf16[256,4096]{1,0:T(8,128)(2,1)}) custom-call(f32[256,2048]{1,0:T(8,128)S(1)} %get-tuple-element.78.kept, bf16[256,2048]{1,0:T(8,128)(2,1)S(1)} %collective-permute-done.28.got, bf16[256,4096]{1,0:T(8,128)(2,1)S(1)} %copy-done.1, bf16[256,4096]{1,0:T(8,128)(2,1)S(1)} %copy-done.2), custom_call_target="tpu_custom_call" | custom-call | flops 5242880 | bytes 7340032 | tf_op jit(solution)/shard_map/pallas_call | solution.py:307
  97.6 2.2 %shard_map.101 = (bf16[256,4096]{1,0:T(8,128)(2,1)}, bf16[256,4096]{1,0:T(8,128)(2,1)}, f32[1,1]{1,0:T(1,128)}) custom-call(f32[256,2048]{1,0:T(8,128)S(1)} %get-tuple-element.75.kept, bf16[256,2048]{1,0:T(8,128)(2,1)S(1)} %collective-permute-done.26.got, bf16[256,4096]{1,0:T(8,128)(2,1)S(1)} %copy-done.1, ...), custom_call_target="tpu_custom_call", output_to_operand_aliasing={{0}: (6, {}), {1}: (7, {})} | custom-call | flops 5242880 | bytes 7340032 | tf_op jit(solution)/shard_map/pallas_call | solution.py:307
  (55 shorter events, 15.3 us)
Async XLA Ops:
  0.6 47.4 %collective-permute-start.15 = (bf16[256,4096]{1,0:T(8,128)(2,1)}, bf16[256,4096]{1,0:T(8,128)(2,1)S(1)}, u32[]{:S(2)}, u32[]{:S(2)}) collective-permute-start(bf16[256,4096]{1,0:T(8,128)(2,1)} %rest_8_.1), channel_id=1, source_target_pairs={{0,1},{1,0},{2,3},{3,2},{4,5},{5,4},{6,7},{7,6},{8,9},{9,8},{10,11... | collective-permute-start | bytes 6291464 | tf_op jit(solution)/shard_map/ppermute | solution.py:402
  1.1 15.3 %collective-permute-start.2 = (bf16[64,4096]{1,0:T(8,128)(2,1)}, bf16[64,4096]{1,0:T(8,128)(2,1)S(1)}, u32[]{:S(2)}, u32[]{:S(2)}) collective-permute-start(bf16[64,4096]{1,0:T(8,128)(2,1)} %rest_0_.1), channel_id=1, source_target_pairs={{0,16},{8,24},{16,0},{24,8},{1,17},{9,25},{17,1},{25,9},{2,18},{10... | collective-permute-start | bytes 1572872 | tf_op jit(solution)/shard_map/ppermute | solution.py:332
  3.7 16.1 %collective-permute-start = (bf16[64,4096]{1,0:T(8,128)(2,1)}, bf16[64,4096]{1,0:T(8,128)(2,1)S(1)}, u32[]{:S(2)}, u32[]{:S(2)}) collective-permute-start(bf16[64,4096]{1,0:T(8,128)(2,1)} %rest_0_.1), channel_id=1, source_target_pairs={{0,2},{2,4},{4,6},{6,0},{1,3},{3,5},{5,7},{7,1},{8,10},{10,12},{12... | collective-permute-start | bytes 1572872 | tf_op jit(solution)/shard_map/ppermute | solution.py:331
  5.3 14.5 %collective-permute-start.3 = (bf16[64,4096]{1,0:T(8,128)(2,1)}, bf16[64,4096]{1,0:T(8,128)(2,1)S(1)}, u32[]{:S(2)}, u32[]{:S(2)}) collective-permute-start(bf16[64,4096]{1,0:T(8,128)(2,1)} %rest_0_.1), channel_id=1, source_target_pairs={{0,8},{8,0},{16,24},{24,16},{1,9},{9,1},{17,25},{25,17},{2,10},{10... | collective-permute-start | bytes 1572872 | tf_op jit(solution)/shard_map/ppermute | solution.py:332
  19.9 12.1 %collective-permute-start.7 = (bf16[48,4096]{1,0:T(8,128)(2,1)S(1)}, bf16[48,4096]{1,0:T(8,128)(2,1)S(1)}, u32[]{:S(2)}, u32[]{:S(2)}) collective-permute-start(bf16[48,4096]{1,0:T(8,128)(2,1)S(1)} %get-tuple-element.49), channel_id=1, source_target_pairs={{0,16},{8,24},{16,0},{24,8},{1,17},{9,25},{17,1},{25,9},{2,18},{10... | collective-permute-start | bytes 1179656 | tf_op jit(solution)/shard_map/ppermute | solution.py:362
  20.5 15.0 %collective-permute-start.1 = (bf16[64,4096]{1,0:T(8,128)(2,1)S(1)}, bf16[64,4096]{1,0:T(8,128)(2,1)S(1)}, u32[]{:S(2)}, u32[]{:S(2)}) collective-permute-start(bf16[64,4096]{1,0:T(8,128)(2,1)S(1)} %collective-permute-done.refs_0_.rest_0_), channel_id=1, source_target_pairs={{0,2},{2,4},{4,6},{6,0},{1,3},{3,5},{5,7},{7,1},{8,10},{10,12},{12... | collective-permute-start | bytes 1572872 | tf_op jit(solution)/shard_map/ppermute | solution.py:331
  21.4 12.1 %collective-permute-start.6 = (bf16[48,4096]{1,0:T(8,128)(2,1)S(1)}, bf16[48,4096]{1,0:T(8,128)(2,1)S(1)}, u32[]{:S(2)}, u32[]{:S(2)}) collective-permute-start(bf16[48,4096]{1,0:T(8,128)(2,1)S(1)} %get-tuple-element.46.refs_3_), channel_id=1, source_target_pairs={{0,8},{8,0},{16,24},{24,16},{1,9},{9,1},{17,25},{25,17},{2,10},{10... | collective-permute-start | bytes 1179656 | tf_op jit(solution)/shard_map/ppermute | solution.py:362
  23.0 17.4 %collective-permute-start.4 = (bf16[48,4096]{1,0:T(8,128)(2,1)S(1)}, bf16[48,4096]{1,0:T(8,128)(2,1)S(1)}, u32[]{:S(2)}, u32[]{:S(2)}) collective-permute-start(bf16[48,4096]{1,0:T(8,128)(2,1)S(1)} %get-tuple-element.47), channel_id=1, source_target_pairs={{0,16},{8,24},{16,0},{24,8},{1,17},{9,25},{17,1},{25,9},{2,18},{10... | collective-permute-start | bytes 1179656 | tf_op jit(solution)/shard_map/ppermute | solution.py:362
  32.0 17.3 %copy-start.5 = (s32[2048]{0:T(1024)S(1)}, s32[2048]{0:T(1024)}, u32[]{:S(2)}) copy-start(s32[2048]{0:T(1024)} %param.11) | copy-start | bytes 24580
  32.0 17.9 %copy-start = (bf16[256,4096]{1,0:T(8,128)(2,1)S(1)}, bf16[256,4096]{1,0:T(8,128)(2,1)}, u32[]{:S(2)}) copy-start(bf16[256,4096]{1,0:T(8,128)(2,1)} %rest_8_.1) | copy-start | bytes 6291460
  32.0 17.9 %copy-start.3 = (bf16[64,4096]{1,0:T(8,128)(2,1)S(1)}, bf16[64,4096]{1,0:T(8,128)(2,1)}, u32[]{:S(2)}) copy-start(bf16[64,4096]{1,0:T(8,128)(2,1)} %rest_0_.1) | copy-start | bytes 1572868
  32.0 9.9 %collective-permute-start.5 = (bf16[48,4096]{1,0:T(8,128)(2,1)S(1)}, bf16[48,4096]{1,0:T(8,128)(2,1)S(1)}, u32[]{:S(2)}, u32[]{:S(2)}) collective-permute-start(bf16[48,4096]{1,0:T(8,128)(2,1)S(1)} %get-tuple-element.48.refs_3_), channel_id=1, source_target_pairs={{0,8},{8,0},{16,24},{24,16},{1,9},{9,1},{17,25},{25,17},{2,10},{10... | collective-permute-start | bytes 1179656 | tf_op jit(solution)/shard_map/ppermute | solution.py:362
  35.5 11.7 %collective-permute-start.13 = (bf16[48,4096]{1,0:T(8,128)(2,1)S(1)}, bf16[48,4096]{1,0:T(8,128)(2,1)S(1)}, u32[]{:S(2)}, u32[]{:S(2)}) collective-permute-start(bf16[48,4096]{1,0:T(8,128)(2,1)S(1)} %get-tuple-element.54), channel_id=1, source_target_pairs={{0,16},{8,24},{16,0},{24,8},{1,17},{9,25},{17,1},{25,9},{2,18},{10... | collective-permute-start | bytes 1179656 | tf_op jit(solution)/shard_map/ppermute | solution.py:362
  36.9 16.7 %collective-permute-start.12 = (bf16[64,4096]{1,0:T(8,128)(2,1)S(1)}, bf16[64,4096]{1,0:T(8,128)(2,1)S(1)}, u32[]{:S(2)}, u32[]{:S(2)}) collective-permute-start(bf16[64,4096]{1,0:T(8,128)(2,1)S(1)} %collective-permute-done.1.refs_0_.rest_0_), channel_id=1, source_target_pairs={{0,2},{2,4},{4,6},{6,0},{1,3},{3,5},{5,7},{7,1},{8,10},{10,12},{12... | collective-permute-start | bytes 1572872 | tf_op jit(solution)/shard_map/ppermute | solution.py:331
  40.4 11.6 %collective-permute-start.14 = (bf16[48,4096]{1,0:T(8,128)(2,1)S(1)}, bf16[48,4096]{1,0:T(8,128)(2,1)S(1)}, u32[]{:S(2)}, u32[]{:S(2)}) collective-permute-start(bf16[48,4096]{1,0:T(8,128)(2,1)S(1)} %get-tuple-element.50.refs_5_), channel_id=1, source_target_pairs={{0,8},{8,0},{16,24},{24,16},{1,9},{9,1},{17,25},{25,17},{2,10},{10... | collective-permute-start | bytes 1179656 | tf_op jit(solution)/shard_map/ppermute | solution.py:362
  42.0 19.7 %collective-permute-start.10 = (bf16[64,4096]{1,0:T(8,128)(2,1)S(1)}, bf16[64,4096]{1,0:T(8,128)(2,1)S(1)}, u32[]{:S(2)}, u32[]{:S(2)}) collective-permute-start(bf16[64,4096]{1,0:T(8,128)(2,1)S(1)} %get-tuple-element.53), channel_id=1, source_target_pairs={{2,0},{4,2},{6,4},{0,6},{3,1},{5,3},{7,5},{1,7},{10,8},{12,10},{14... | collective-permute-start | bytes 1572872 | tf_op jit(solution)/shard_map/ppermute | solution.py:357
  47.3 14.8 %collective-permute-start.9 = (bf16[48,4096]{1,0:T(8,128)(2,1)S(1)}, bf16[48,4096]{1,0:T(8,128)(2,1)S(1)}, u32[]{:S(2)}, u32[]{:S(2)}) collective-permute-start(bf16[48,4096]{1,0:T(8,128)(2,1)S(1)} %get-tuple-element.52), channel_id=1, source_target_pairs={{0,16},{8,24},{16,0},{24,8},{1,17},{9,25},{17,1},{25,9},{2,18},{10... | collective-permute-start | bytes 1179656 | tf_op jit(solution)/shard_map/ppermute | solution.py:362
  48.0 15.1 %collective-permute-start.8 = (bf16[48,4096]{1,0:T(8,128)(2,1)S(1)}, bf16[48,4096]{1,0:T(8,128)(2,1)S(1)}, u32[]{:S(2)}, u32[]{:S(2)}) collective-permute-start(bf16[48,4096]{1,0:T(8,128)(2,1)S(1)} %get-tuple-element.51.refs_3_), channel_id=1, source_target_pairs={{0,8},{8,0},{16,24},{24,16},{1,9},{9,1},{17,25},{25,17},{2,10},{10... | collective-permute-start | bytes 1179656 | tf_op jit(solution)/shard_map/ppermute | solution.py:362
  53.7 12.7 %collective-permute-start.19 = (bf16[48,4096]{1,0:T(8,128)(2,1)S(1)}, bf16[48,4096]{1,0:T(8,128)(2,1)S(1)}, u32[]{:S(2)}, u32[]{:S(2)}) collective-permute-start(bf16[48,4096]{1,0:T(8,128)(2,1)S(1)} %get-tuple-element.57), channel_id=1, source_target_pairs={{0,16},{8,24},{16,0},{24,8},{1,17},{9,25},{17,1},{25,9},{2,18},{10... | collective-permute-start | bytes 1179656 | tf_op jit(solution)/shard_map/ppermute | solution.py:362
  54.4 12.2 %collective-permute-start.18 = (bf16[48,4096]{1,0:T(8,128)(2,1)S(1)}, bf16[48,4096]{1,0:T(8,128)(2,1)S(1)}, u32[]{:S(2)}, u32[]{:S(2)}) collective-permute-start(bf16[48,4096]{1,0:T(8,128)(2,1)S(1)} %get-tuple-element.56.refs_1_), channel_id=1, source_target_pairs={{0,8},{8,0},{16,24},{24,16},{1,9},{9,1},{17,25},{25,17},{2,10},{10... | collective-permute-start | bytes 1179656 | tf_op jit(solution)/shard_map/ppermute | solution.py:362
  61.8 8.3 %collective-permute-start.11 = (bf16[32,4096]{1,0:T(8,128)(2,1)S(1)}, bf16[32,4096]{1,0:T(8,128)(2,1)S(1)}, u32[]{:S(2)}, u32[]{:S(2)}) collective-permute-start(bf16[32,4096]{1,0:T(8,128)(2,1)S(1)} %shard_map.90), channel_id=1, source_target_pairs={{2,0},{4,2},{6,4},{0,6},{3,1},{5,3},{7,5},{1,7},{10,8},{12,10},{14... | collective-permute-start | bytes 786440 | tf_op jit(solution)/shard_map/ppermute | solution.py:360
  62.1 8.8 %collective-permute-start.17 = (bf16[32,4096]{1,0:T(8,128)(2,1)S(1)}, bf16[32,4096]{1,0:T(8,128)(2,1)S(1)}, u32[]{:S(2)}, u32[]{:S(2)}) collective-permute-start(bf16[32,4096]{1,0:T(8,128)(2,1)S(1)} %shard_map.93), channel_id=1, source_target_pairs={{0,16},{8,24},{16,0},{24,8},{1,17},{9,25},{17,1},{25,9},{2,18},{10... | collective-permute-start | bytes 786440 | tf_op jit(solution)/shard_map/ppermute | solution.py:362
  63.1 8.4 %collective-permute-start.16 = (bf16[32,4096]{1,0:T(8,128)(2,1)S(1)}, bf16[32,4096]{1,0:T(8,128)(2,1)S(1)}, u32[]{:S(2)}, u32[]{:S(2)}) collective-permute-start(bf16[32,4096]{1,0:T(8,128)(2,1)S(1)} %shard_map.93), channel_id=1, source_target_pairs={{0,8},{8,0},{16,24},{24,16},{1,9},{9,1},{17,25},{25,17},{2,10},{10... | collective-permute-start | bytes 786440 | tf_op jit(solution)/shard_map/ppermute | solution.py:362
  73.7 3.7 %collective-permute-start.22 = (f32[4,2,2,128]{3,2,1,0:T(2,128)S(1)}, f32[4,2,2,128]{3,2,1,0:T(2,128)S(1)}, u32[]{:S(2)}, u32[]{:S(2)}) collective-permute-start(f32[4,2,2,128]{3,2,1,0:T(2,128)S(1)} %get-tuple-element.61.refs_0_), channel_id=1, source_target_pairs={{0,6},{2,0},{4,2},{6,4},{1,7},{3,1},{5,3},{7,5},{8,14},{10,8},{12,... | collective-permute-start | bytes 24584 | tf_op jit(solution)/shard_map/ppermute | solution.py:26
  75.9 4.5 %collective-permute-start.21 = (f32[4,2,2,128]{3,2,1,0:T(2,128)S(1)}, f32[4,2,2,128]{3,2,1,0:T(2,128)S(1)}, u32[]{:S(2)}, u32[]{:S(2)}) collective-permute-start(f32[4,2,2,128]{3,2,1,0:T(2,128)S(1)} %get-tuple-element.61.refs_0_), channel_id=1, source_target_pairs={{0,4},{2,6},{4,0},{6,2},{1,5},{3,7},{5,1},{7,3},{8,12},{10,14},{12... | collective-permute-start | bytes 24584 | tf_op jit(solution)/shard_map/ppermute | solution.py:26
  76.2 5.4 %collective-permute-start.20 = (f32[4,2,2,128]{3,2,1,0:T(2,128)S(1)}, f32[4,2,2,128]{3,2,1,0:T(2,128)S(1)}, u32[]{:S(2)}, u32[]{:S(2)}) collective-permute-start(f32[4,2,2,128]{3,2,1,0:T(2,128)S(1)} %get-tuple-element.61.refs_0_), channel_id=1, source_target_pairs={{0,2},{2,4},{4,6},{6,0},{1,3},{3,5},{5,7},{7,1},{8,10},{10,12},{12... | collective-permute-start | bytes 24584 | tf_op jit(solution)/shard_map/ppermute | solution.py:26
  81.7 3.7 %collective-permute-start.25 = (f32[4,2,2,128]{3,2,1,0:T(2,128)S(1)}, f32[4,2,2,128]{3,2,1,0:T(2,128)S(1)}, u32[]{:S(2)}, u32[]{:S(2)}) collective-permute-start(f32[4,2,2,128]{3,2,1,0:T(2,128)S(1)} %shard_map.97.refs_0_), channel_id=1, source_target_pairs={{0,24},{8,0},{16,8},{24,16},{1,25},{9,1},{17,9},{25,17},{2,26},{10... | collective-permute-start | bytes 24584 | tf_op jit(solution)/shard_map/ppermute | solution.py:26
  83.8 3.7 %collective-permute-start.24 = (f32[4,2,2,128]{3,2,1,0:T(2,128)S(1)}, f32[4,2,2,128]{3,2,1,0:T(2,128)S(1)}, u32[]{:S(2)}, u32[]{:S(2)}) collective-permute-start(f32[4,2,2,128]{3,2,1,0:T(2,128)S(1)} %shard_map.97.refs_0_), channel_id=1, source_target_pairs={{0,16},{8,24},{16,0},{24,8},{1,17},{9,25},{17,1},{25,9},{2,18},{10... | collective-permute-start | bytes 24584 | tf_op jit(solution)/shard_map/ppermute | solution.py:26
  84.2 4.6 %collective-permute-start.23 = (f32[4,2,2,128]{3,2,1,0:T(2,128)S(1)}, f32[4,2,2,128]{3,2,1,0:T(2,128)S(1)}, u32[]{:S(2)}, u32[]{:S(2)}) collective-permute-start(f32[4,2,2,128]{3,2,1,0:T(2,128)S(1)} %shard_map.97.refs_0_), channel_id=1, source_target_pairs={{0,8},{8,16},{16,24},{24,0},{1,9},{9,17},{17,25},{25,1},{2,10},{10... | collective-permute-start | bytes 24584 | tf_op jit(solution)/shard_map/ppermute | solution.py:26
  91.7 3.6 %collective-permute-start.28 = (bf16[256,2048]{1,0:T(8,128)(2,1)S(1)}, bf16[256,2048]{1,0:T(8,128)(2,1)S(1)}, u32[]{:S(2)}, u32[]{:S(2)}) collective-permute-start(bf16[256,2048]{1,0:T(8,128)(2,1)S(1)} %get-tuple-element.79), channel_id=1, source_target_pairs={{0,1},{1,0},{2,3},{3,2},{4,5},{5,4},{6,7},{7,6},{8,9},{9,8},{10,11... | collective-permute-start | bytes 3145736 | tf_op jit(solution)/shard_map/ppermute | solution.py:438
  94.7 2.8 %collective-permute-start.26 = (bf16[256,2048]{1,0:T(8,128)(2,1)S(1)}, bf16[256,2048]{1,0:T(8,128)(2,1)S(1)}, u32[]{:S(2)}, u32[]{:S(2)}) collective-permute-start(bf16[256,2048]{1,0:T(8,128)(2,1)S(1)} %get-tuple-element.76), channel_id=1, source_target_pairs={{0,1},{1,0},{2,3},{3,2},{4,5},{5,4},{6,7},{7,6},{8,9},{9,8},{10,11... | collective-permute-start | bytes 3145736 | tf_op jit(solution)/shard_map/ppermute | solution.py:438
  95.3 2.3 %collective-permute-start.27 = (f32[4,2,1,128]{3,2,1,0:T(1,128)S(1)}, f32[4,2,1,128]{3,2,1,0:T(1,128)S(1)}, u32[]{:S(2)}, u32[]{:S(2)}) collective-permute-start(f32[4,2,1,128]{3,2,1,0:T(1,128)S(1)} %get-tuple-element.77.rest_0_), channel_id=1, source_target_pairs={{0,1},{1,0},{2,3},{3,2},{4,5},{5,4},{6,7},{7,6},{8,9},{9,8},{10,11... | collective-permute-start | bytes 12296 | tf_op jit(solution)/shard_map/ppermute | solution.py:439
  (3 other events, 24.4 us)
